TPU v7x, 512 devices: a whole 4x8x8 slice. The times are simulated.
512 devices in a mesh: cube: 4 (over x), row: 8 (over y), col: 16 (over z, core).
Axes of the slice: x: 4, y: 8, z: 8, core: 2. Of those that a mesh axis runs over, the one named last changes fastest.
Arguments:
- front_tiles: float32 [3, 32, 256, 2, 16, 256], P(None, ('cube', 'row'), None, None, 'col'), may hold values from -1 to 64, as said below
- child_tiles: bfloat16 [4, 8, 16, 4, 256, 256], P('cube', 'row', 'col'), may hold values from -0.5 to 0.5
- target_rows: int32 [4, 8, 16, 4], P('cube', 'row', 'col'), may hold values from 0 to 95, as said below
- target_cols: int32 [4, 8, 16, 4], P('cube', 'row', 'col'), may hold values from 0 to 31, as said below
- live_counts: int32 [4, 8, 16], P('cube', 'row', 'col'), may hold values from 1 to 4, as said below
Outputs:
- factored: float32 [3, 32, 256, 2, 16, 256], P(None, ('cube', 'row'), None, None, 'col')
Inputs may be any that keep to these rules, and one draw needn't show every extreme that they name: `live_counts`: some device holds 4 live slots in every draw. target_rows[c, r, q, m] leaves remainder r on division by the row axis's size. Call the owning cube index of a parent tile row its remainder modulo 32, divided by the row axis's size: of one device's live slots at most 2 have one owning cube index, and in every draw some owner receives 2 live slots from every device that shares its row and col indices. target_cols[c, r, q, m] leaves remainder q on division by 16. `front_tiles`: after assembly the symmetric part of tile (0, 0) is positive definite.
All inputs are finite; a program needn't handle non-finite values.
Results may differ from a plain program's by a relative error of at most 0.0003.
Values may be sent and summed in bfloat16 or wider, within the bound.
A program may use at most 64 MiB of HBM per device.

v0:
```python
import jax
import jax.numpy as jnp
from jax import lax
from jax.sharding import PartitionSpec as P

HIGHEST_PREC = lax.Precision.HIGHEST


def from_root(value, axis, source):
    kept = jnp.where(lax.axis_index(axis) == source, value, 0).astype(value.dtype)
    return lax.psum(kept, axis)


def spread_tiles(addresses, how_many, tile_values):
    picker = (addresses[None, :] == jnp.arange(how_many, dtype=jnp.int32)[:, None]).astype(
        tile_values.dtype
    )
    return jnp.einsum("mn,nab->mab", picker, tile_values, preferred_element_type=jnp.float32)


def local(front_tiles, child_tiles, target_rows, target_cols, live_counts):
    across = lax.axis_size("row")
    groups = lax.axis_size("cube") * across
    columns = lax.axis_size("col")
    row_tiles = front_tiles.shape[0]
    tile_width = front_tiles.shape[2]
    col_tiles = front_tiles.shape[3]
    slot_count = child_tiles.shape[3]
    owned_count = row_tiles * col_tiles
    initial = (
        front_tiles.reshape(row_tiles, tile_width, col_tiles, tile_width)
        .transpose(0, 2, 1, 3)
        .reshape(owned_count, tile_width, tile_width)
    )
    slot_values = child_tiles.reshape(slot_count, tile_width, tile_width)
    parent_rows = target_rows.reshape(slot_count)
    parent_cols = target_cols.reshape(slot_count)
    slot_alive = jnp.arange(slot_count, dtype=jnp.int32) < live_counts.reshape(())
    dest_cube = parent_rows % groups // across
    dest_tile = parent_rows // groups * col_tiles + parent_cols // columns
    routed = jnp.where(slot_alive, dest_cube * owned_count + dest_tile, -1)
    home_base = lax.axis_index("cube") * owned_count
    arrivals = spread_tiles(
        lax.all_gather(routed, "cube", axis=0, tiled=True) - home_base,
        owned_count,
        lax.all_gather(slot_values, "cube", axis=0, tiled=True),
    )
    assembled = (initial + arrivals).reshape(row_tiles, col_tiles, tile_width, tile_width)
    first_column = assembled[:, 0]
    panel_raw = from_root(first_column, "col", 0)
    corner = from_root(panel_raw[0], ("cube", "row"), 0)
    factor = jnp.linalg.cholesky(0.5 * (corner + corner.T))
    solved = lax.linalg.triangular_solve(
        jnp.broadcast_to(factor, panel_raw.shape),
        panel_raw,
        left_side=False,
        lower=True,
        transpose_a=True,
    )
    grid_row = lax.axis_index("cube") * across + lax.axis_index("row")
    global_rows = jnp.arange(row_tiles, dtype=jnp.int32) * groups + grid_row
    panel_tiles = jnp.where(global_rows[:, None, None] == 0, factor[None], solved)
    column_here = lax.axis_index("col")
    picked = []
    for window in range(col_tiles):
        wanted = window * columns + column_here
        holder = wanted % groups
        chosen = lax.dynamic_index_in_dim(panel_tiles, wanted // groups, 0, keepdims=False)
        picked.append(from_root(chosen, ("cube", "row"), holder))
    transposed = jnp.stack(picked)
    update = jnp.einsum("iab,jcb->ijac", panel_tiles, transposed, precision=HIGHEST_PREC)
    global_cols = jnp.arange(col_tiles, dtype=jnp.int32) * columns + column_here
    trailing = assembled - update
    result = jnp.where(
        global_cols[None, :, None, None] == 0,
        panel_tiles[:, None],
        jnp.where(global_rows[:, None, None, None] == 0, jnp.zeros_like(trailing), trailing),
    )
    return result.transpose(0, 2, 1, 3).reshape(front_tiles.shape)


def solution(mesh):
    placed = (
        P(None, ("cube", "row"), None, None, "col", None),
        P("cube", "row", "col", None, None, None),
        P("cube", "row", "col", None),
        P("cube", "row", "col", None),
        P("cube", "row", "col"),
    )
    return jax.shard_map(
        local,
        mesh=mesh,
        in_specs=placed,
        out_specs=P(None, ("cube", "row"), None, None, "col", None),
        check_vma=False,
    )
```

profile of v0, /device:TPU:65, one launch (start us, length us, event | category | flops | bytes accessed | tf_op | source)
XLA Modules:
  0.0 601.2 jit_solution(14055543509564479123)
XLA Ops:
  6.5 0.7 all-gather.3.cloned.1.call-update
  8.0 1.6 copy.63
  9.5 1.3 dynamic-slice.4
  11.6 6.9 %all-reduce.1 = s32[16]{0:T(128)S(1)} all-reduce(s32[16]{0:T(128)S(1)} %fusion.23), channel_id=1, replica_groups=mesh['cube'=4,'row'=8,'col'=16] {'cube'}, use_global_device_ids=true, to_apply=%add.1 | all-reduce | flops 16 | bytes 128
  18.5 31.1 %all-gather.3.cloned.1.call-done = bf16[1,1,1,16,256,256]{5,4,2,1,0,3:T(8,128)(2,1)} async-done(((bf16[1,1,1,4,256,256]{5,4,2,1,0,3:T(8,128)(2,1)}), bf16[1,1,1,16,256,256]{5,4,2,1,0,3:T(8,128)(2,1)}) %all-gather.3.cloned.1.call-update) | async-done | bytes 2097168 | tf_op jit(solution)/shard_map/all_gather | solution.py:46
  49.6 2.8 fusion
  52.4 0.5 bitcast_add_fusion
  53.0 0.5 copy.67
  53.5 0.9 fusion.6
  54.5 114.8 %all-reduce.7.cloned.1.call-done = f32[3,256,256]{1,2,0:T(8,128)} async-done(((f32[3,256,256]{1,2,0:T(8,128)}), f32[3,256,256]{1,2,0:T(8,128)}) %all-reduce.7.cloned.1.call-update) | async-done | bytes 786448 | tf_op jit(solution)/shard_map/psum | solution.py:11
  169.3 1.7 fusion.12
  171.5 154.4 %all-reduce.9.cloned.1.call-done = f32[256,256]{0,1:T(8,128)} async-done(((f32[256,256]{0,1:T(8,128)}), f32[256,256]{0,1:T(8,128)}) %all-reduce.9.cloned.1.call-update) | async-done | bytes 262160 | tf_op jit(solution)/shard_map/psum | solution.py:11
  325.9 1.1 copy.68
  327.0 1.0 fusion.14
  328.1 11.7 %cholesky.49 = f32[128,128]{1,0:T(8,128)S(1)} custom-call(f32[128,128]{1,0:T(8,128)S(1)} %cholesky.115), custom_call_target="Cholesky" | custom-call | tf_op jit(solution)/shard_map/jit(cholesky)/cholesky | solution.py:52
  339.9 9.8 %custom-call.14 = f32[1,128,128]{1,2,0:T(8,128)S(1)} custom-call(f32[1,128,128]{2,1,0:T(8,128)S(1)} %get-tuple-element.46), custom_call_target="InvertDiagBlocksLowerTriangular" | custom-call | tf_op jit(solution)/shard_map/jit(cholesky)/cholesky | solution.py:52
  350.2 11.7 %cholesky.103 = f32[128,128]{1,0:T(8,128)S(1)} custom-call(f32[128,128]{1,0:T(8,128)S(1)} %convolution_subtract_fusion.1), custom_call_target="Cholesky" | custom-call | tf_op jit(solution)/shard_map/jit(cholesky)/cholesky | solution.py:52
  362.0 0.6 compare_reduce_fusion
  364.1 4.3 while.1
  364.3 0.6 fusion.31
  364.9 1.3 constant_dynamic-slice_fusion.5
  366.4 0.6 fusion.31
  367.0 1.3 constant_dynamic-slice_fusion.5
  368.5 59.0 %custom-call.15 = f32[3,2,128,128]{2,3,1,0:T(8,128)S(1)} custom-call(f32[3,2,128,128]{3,2,1,0:T(8,128)S(1)} %bitcast.104), custom_call_target="InvertDiagBlocksLowerTriangular" | custom-call | tf_op jit(solution)/shard_map/triangular_solve | solution.py:53
  427.5 1.5 fusion.10
  429.0 1.5 convolution_subtract_fusion
  430.5 0.5 fusion.15
  431.2 0.9 copy-done
  432.1 0.8 dynamic-slice_select_fusion.1
  433.0 155.8 %all-reduce.11.cloned.1.call-done = (f32[1,256,256]{1,2,0:T(8,128)}, f32[1,256,256]{1,2,0:T(8,128)}) async-done(((f32[1,256,256]{1,2,0:T(8,128)}, f32[1,256,256]{1,2,0:T(8,128)}), (f32[1,256,256]{1,2,0:T(8,128)}, f32[1,256,256]{1,2,0:T(8,128)})) %all-reduce.11.cloned.1.call-update) | async-done | bytes 524304 | tf_op jit(solution)/shard_map/psum | solution.py:11
  588.7 3.1 fusion.5
  591.9 2.7 copy.84
  (40 shorter events, 2.2 us)
Async XLA Ops:
  6.5 43.0 %all-gather.3.cloned.1.call-start = ((), (), s32[]{:S(2)}) async-start(), calls=%async_computation.2 | async-start | bytes 2621440 | tf_op jit(solution)/shard_map/all_gather | solution.py:46
  7.3 162.0 %all-reduce.7.cloned.1.call-start = ((), (), s32[]{:S(2)}) async-start(), calls=%async_computation | async-start | bytes 1572864 | tf_op jit(solution)/shard_map/psum | solution.py:11
  8.0 3.5 copy-start.1
  8.0 3.5 copy-start.2
  54.4 271.5 %all-reduce.9.cloned.1.call-start = ((), (), s32[]{:S(2)}) async-start(), calls=%async_computation.1 | async-start | bytes 524288 | tf_op jit(solution)/shard_map/psum | solution.py:11
  171.0 417.8 %all-reduce.11.cloned.1.call-start = ((), (), s32[]{:S(2)}) async-start(), calls=%async_computation.3 | async-start | bytes 1048576 | tf_op jit(solution)/shard_map/psum | solution.py:11
  431.2 0.9 copy-start
Sparse Core Ops, SparseCore 0:
  9.5 40.0 all-gather.2
  54.5 114.6 all-reduce.6
  173.1 152.7 all-reduce.8
  433.1 155.6 all-reduce.10
where the time goes:
time: 606 us; the launch traced here: 601 us
  waiting for transfers between devices  457 us (75%)
  other arithmetic  98.4 us (16%)
  between operations  16 us (3%)
  local copies, waits for them, and re-layouts  12.6 us (2%)
  matrix products  10 us (2%)
  blocking collectives  6.86 us (1%)
    psum x3, waiting for transfers between devices, from_root(): return lax.psum(kept, axis)  425 us
    another operation x3, other arithmetic, local(): lax.linalg.triangular_solve(jnp.broadcast_to(factor, panel_raw.shape), pa...  59 us
    another operation x6, other arithmetic, local(): factor = jnp.linalg.cholesky(0.5 * (corner + corner.T))  33.9 us
    all_gather x1, waiting for transfers between devices, local(): lax.all_gather(slot_values, 'cube', axis=0, tiled=True)  31.1 us
  transfers between devices with their start and end apart: 4, of which 4 were waited for; matrix products, arithmetic and copies ran while one was open for 1% of the time, Pallas kernels for 0%

commit v1 on v0

v1 whole, which is shorter than its diff:
```python
import jax
import jax.numpy as jnp
from jax import lax
from jax.experimental import pallas as pl
from jax.experimental.pallas import tpu as pltpu
from jax.sharding import PartitionSpec as P

MESH = pl.DeviceIdType.MESH
HIGHEST = lax.Precision.HIGHEST
F32 = jnp.float32
BF16 = jnp.bfloat16

NX, NY, NZ = 4, 8, 8
OWNERS = NX * NY
NCOL = 2 * NZ
TILE = 256
TR = 3
SLOTS = 4
LANES = 2
META = LANES * TILE
STAGE_ROWS = META + 16
PIECE = TILE // OWNERS
ZPIECE = TILE // NZ
NB = 32
NCHUNK = TILE // NB


def nt(a, b):
    return lax.dot_general(a, b, (((1,), (1,)), ((), ())), precision=HIGHEST, preferred_element_type=F32)


def drain(view, sem, times=1):
    for _ in range(times):
        pltpu.make_async_copy(view, view, sem).wait()


def cholesky_step(b, m_ref, u_ref, w_ref):
    row0 = pl.multiple_of(b * NB, NB)
    block = m_ref[pl.ds(row0, NB), :]
    half = jnp.where(b < NCHUNK // 2, block[:, :128], block[:, 128:256])
    diag = pltpu.roll(half, lax.rem(128 - lax.rem(b * NB, 128), 128), 1)
    parts = [block[:, 128 * i : 128 * (i + 1)] for i in range(4)] + [diag]
    rows = lax.broadcasted_iota(jnp.int32, (NB, 128), 0)
    for g in range(NB // 8):
        base = 8 * g
        cols = [jnp.broadcast_to(parts[4][base:, base + j : base + j + 1], (NB - base, 128)) for j in range(8)]
        live = [p[base:] for p in parts]
        below = rows[base:] - base
        for kk in range(8):
            pivot = cols[kk][kk : kk + 1, :]
            inv = lax.rsqrt(pivot)
            inv = inv * (1.5 - 0.5 * pivot * inv * inv)
            col = cols[kk] * inv
            masked = jnp.where(below > kk, col, 0.0)
            for j in range(kk + 1, 8):
                cols[j] = cols[j] - masked * col[j : j + 1, :]
            for i in range(5):
                top = live[i][kk : kk + 1, :] * inv
                live[i] = jnp.where(below == kk, top, live[i] - masked * top)
        parts = [l if g == 0 else jnp.concatenate([p[:base], l], axis=0) for p, l in zip(parts, live)]
    u = jnp.concatenate(parts[:2], axis=1)
    winv = jnp.concatenate(parts[2:4], axis=1)
    u_ref[pl.ds(row0, NB), :] = u
    w_ref[pl.ds(row0, NB), :] = winv
    both = jnp.concatenate(parts[:4], axis=1)
    b1 = both.astype(BF16)
    rest = both - b1.astype(F32)
    b2 = rest.astype(BF16)
    b3 = (rest - b2.astype(F32)).astype(BF16)
    a1, a2, a3 = b1[:, :TILE], b2[:, :TILE], b3[:, :TILE]
    lhs = jnp.concatenate([a1, a1, a2, a2, a1, a3], axis=0)
    rhs = jnp.concatenate([b1, b2, b1, b2, b3, b1], axis=0)
    m_ref[...] -= lax.dot_general(lhs, rhs, (((0,), (0,)), ((), ())), preferred_element_type=F32)


def kernel(
    front, child, trow, tcol, live, out,
    stage, recv, asm, brow, bcol, w, m_ref, u_ref,
    ch_s, ch_r, cs_s, cs_r, ca_s, ca_r, rs_s, rs_r, ra_s, ra_r, rf_s, rf_r, w_s, w_r,
):
    x, y, q = lax.axis_index("cube"), lax.axis_index("row"), lax.axis_index("col")
    z, h = q // 2, q % 2
    k = x * NY + y
    is_root = (k == 0) & (q == 0)
    is_helper = (k == 0) & (q == 1)

    def at(xx, yy, zz, hh):
        return (xx, yy, zz * 2 + hh)

    def send(src, dst, ssem, rsem, device):
        pltpu.make_async_remote_copy(
            src_ref=src, dst_ref=dst, send_sem=ssem, recv_sem=rsem, device_id=device, device_id_type=MESH
        ).start()

    my_s, my_q = k // NCOL, k % NCOL
    my_z, my_h = my_q // 2, my_q % 2

    barrier = pltpu.get_barrier_semaphore()

    def greet(device):
        pl.semaphore_signal(barrier, inc=1, device_id=device, device_id_type=MESH)

    def greet_plane(i, c):
        p = lax.rem(k + i, OWNERS)
        greet(at(p // NY, lax.rem(p, NY), z, h))
        return c

    def greet_z(i, c):
        greet(at(x, y, lax.rem(z + i, NZ), h))
        return c

    lax.fori_loop(1, NX * NY, greet_plane, 0)
    lax.fori_loop(1, NZ, greet_z, 0)
    greet(at(x, y, z, 1 - h))

    for s in range(2):
        owner = s * NCOL + q
        @pl.when((owner != 0) & jnp.logical_not((owner == k) & (q == 0)))
        def _():
            greet(at(owner // NY, lax.rem(owner, NY), 0, 0))

    alive = [jnp.where(m < live[0], 1, 0) for m in range(SLOTS)]
    cube_of = [lax.rem(trow[m], OWNERS) // NY for m in range(SLOTS)]
    tile_of = [(trow[m] // OWNERS) * 2 + tcol[m] // NCOL for m in range(SLOTS)]
    meta_row = lax.broadcasted_iota(jnp.int32, (16, TILE), 0)
    for d in range(NX):
        seen = 0
        index = [0, 0]
        label = [-1, -1]
        for m in range(SLOTS):
            hit = alive[m] * jnp.where(cube_of[m] == d, 1, 0)
            for lane in range(LANES):
                here = hit * jnp.where(seen == lane, 1, 0)
                index[lane] = index[lane] + here * m
                label[lane] = label[lane] + here * (tile_of[m] + 1)
            seen = seen + hit
        for lane in range(LANES):
            stage[d, lane * TILE : (lane + 1) * TILE, :] = child[index[lane]]
        tags = jnp.where(meta_row == 0, label[0], jnp.where(meta_row == 1, label[1], -1))
        stage[d, META:, :] = tags.astype(F32).astype(BF16)

    w[: TILE // 2, TILE // 2 :] = jnp.zeros((TILE // 2, TILE // 2), F32)

    greeted_by_column = jnp.where((q != 0) | (k == 0), 0, jnp.where(k == NCOL, OWNERS - 1, OWNERS))
    pl.semaphore_wait(barrier, NX * NY - 1 + NZ - 1 + 1 + greeted_by_column)

    for i in range(1, NX):
        d = lax.rem(x + i, NX)
        send(stage.at[d], recv.at[x], ch_s.at[i], ch_r.at[x], at(d, y, z, h))
    recv[x] = stage[x]

    def wait_children():
        for i in range(1, NX):
            src = lax.rem(x + i, NX)
            drain(recv.at[src], ch_r.at[src])

    def assemble(t, s, dst):
        tile_id = (t * 2 + s).astype(F32) if hasattr(t, "astype") else float(t * 2 + s)
        masks = []
        for src in range(NX):
            tags = recv[src, META:, :].astype(F32)
            masks.append([tags[lane : lane + 1, :] == tile_id for lane in range(LANES)])

        def rows(i, c):
            r0 = pl.multiple_of(i * 32, 32)
            start = t * (TILE * 4) + i * 128 + 2 * s
            acc = jnp.concatenate(
                [front[pl.ds(start, 32, stride=4), :], front[pl.ds(start + 1, 32, stride=4), :]], axis=1
            )
            for src in range(NX):
                for lane in range(LANES):
                    v = recv[src, pl.ds(lane * TILE + r0, 32), :].astype(F32)
                    acc = acc + jnp.where(masks[src][lane], v, 0.0)
            dst[pl.ds(r0, 32), :] = acc
            return c

        lax.fori_loop(0, TILE // 32, rows, 0)

    @pl.when(q == 0)
    def _():
        wait_children()
        assemble(0, 0, brow.at[0])

        @pl.when(k != 0)
        def _():
            def scatter(p, c):
                view = pl.ds(pl.multiple_of(p * PIECE, PIECE), PIECE)
                @pl.when((p != k) | (my_q != 0))
                def _():
                    send(brow.at[0, view, :], bcol.at[my_s, view, :], cs_s, cs_r.at[my_s],
                         at(p // NY, lax.rem(p, NY), my_z, my_h))
                return c

            lax.fori_loop(0, OWNERS, scatter, 0)

        @pl.when(k == NCOL)
        def _():
            bcol[1, NCOL * PIECE : (NCOL + 1) * PIECE, :] = brow[0, NCOL * PIECE : (NCOL + 1) * PIECE, :]

        for t in range(1, TR):
            assemble(t, 0, brow.at[t])

        def spread(p, c):
            view = pl.ds(pl.multiple_of(p * ZPIECE, ZPIECE), ZPIECE)
            send(brow.at[:, view, :], brow.at[:, view, :], rs_s, rs_r, at(x, y, p, 0))
            send(brow.at[:, 0:ZPIECE, :], brow.at[:, 0:ZPIECE, :], ra_s, ra_r.at[0], at(x, y, p, 0))
            return c

        lax.fori_loop(1, NZ, spread, 0)
        send(brow, brow, rf_s, rf_r, at(x, y, 0, 1))

    @pl.when(is_root)
    def _():
        a = brow[0]
        m_ref[:, :TILE] = 0.5 * (a + a.T)
        ii = lax.broadcasted_iota(jnp.int32, (TILE, TILE), 0)
        jj = lax.broadcasted_iota(jnp.int32, (TILE, TILE), 1)
        m_ref[:, TILE:] = jnp.where(ii == jj, 1.0, 0.0)

        def narrow(b, c):
            cholesky_step(b, m_ref, u_ref, w)
            view = pl.ds(pl.multiple_of(b * NB, NB), NB)
            send(w.at[view, 0:128], w.at[view, 0:128], w_s, w_r.at[b], at(0, 0, 0, 1))
            return c

        def wide(b, c):
            cholesky_step(b, m_ref, u_ref, w)
            view = pl.ds(pl.multiple_of(b * NB, NB), NB)
            send(w.at[view, :], w.at[view, :], w_s, w_r.at[b], at(0, 0, 0, 1))
            return c

        lax.fori_loop(0, NCHUNK // 2, narrow, 0)
        lax.fori_loop(NCHUNK // 2, NCHUNK, wide, 0)

    @pl.when(q != 0)
    def _():
        drain(bcol.at[0, 0:PIECE, :], cs_r.at[0])

    @pl.when(jnp.logical_not((q == 0) & (k == NCOL)))
    def _():
        drain(bcol.at[0, 0:PIECE, :], cs_r.at[1])

    mine = pl.ds(pl.multiple_of(k * PIECE, PIECE), PIECE)

    def gather_columns(i, c):
        p = lax.rem(k + i, OWNERS)
        send(bcol.at[:, mine, :], bcol.at[:, mine, :], ca_s, ca_r, at(p // NY, lax.rem(p, NY), z, h))
        return c

    lax.fori_loop(1, OWNERS, gather_columns, 0)

    @pl.when((h == 0) & (z != 0))
    def _():
        drain(brow.at[:, 0:ZPIECE, :], rs_r)
        view = pl.ds(pl.multiple_of(z * ZPIECE, ZPIECE), ZPIECE)

        def gather_rows(i, c):
            to = lax.rem(z + i, NZ)
            @pl.when(to != 0)
            def _():
                send(brow.at[:, view, :], brow.at[:, view, :], ra_s, ra_r.at[z], at(x, y, to, 0))
            return c

        lax.fori_loop(1, NZ, gather_rows, 0)

    @pl.when(q != 0)
    def _():
        wait_children()

        def all_rows(t, c):
            assemble(t, 0, asm.at[0, t])
            return c

        lax.fori_loop(0, TR, all_rows, 0)

    def second_rows(t, c):
        assemble(t, 1, asm.at[1, t])
        return c

    lax.fori_loop(0, TR, second_rows, 0)

    @pl.when((h == 0) & (z != 0))
    def _():
        def one(i, c):
            frm = lax.rem(z + i, NZ)
            drain(brow.at[:, 0:ZPIECE, :], ra_r.at[frm])
            return c

        lax.fori_loop(1, NZ, one, 0)
        send(brow, brow, rf_s, rf_r, at(x, y, z, 1))

    def pass_on(b, part):
        @pl.when((k == 0) & (z == 0))
        def _():
            for i in range(1, NX):
                send(part, part, w_s, w_r.at[b], at(i, 0, 0, 1))

        @pl.when((y == 0) & (z == 0))
        def _():
            for i in range(1, NY):
                send(part, part, w_s, w_r.at[b], at(x, i, 0, 1))

        @pl.when(z == 0)
        def _():
            for i in range(1, NZ):
                send(part, part, w_s, w_r.at[b], at(x, y, i, 1))

        @pl.when(jnp.logical_not(is_helper))
        def _():
            send(part, part, w_s, w_r.at[b], at(x, y, z, 0))

    def narrow_part(b):
        return w.at[pl.ds(pl.multiple_of(b * NB, NB), NB), 0:128]

    def wide_part(b):
        return w.at[pl.ds(pl.multiple_of(b * NB, NB), NB), :]

    @pl.when(jnp.logical_not(is_root))
    def _():
        def narrow(b, c):
            drain(narrow_part(b), w_r.at[b])
            @pl.when(h == 1)
            def _():
                pass_on(b, narrow_part(b))
            return c

        def wide(b, c):
            drain(wide_part(b), w_r.at[b])
            @pl.when(h == 1)
            def _():
                pass_on(b, wide_part(b))
            return c

        lax.fori_loop(0, NCHUNK // 2, narrow, 0)
        lax.fori_loop(NCHUNK // 2, NCHUNK, wide, 0)

    drain(bcol.at[:, 0 : TILE - PIECE, :], ca_r)

    @pl.when(h == 1)
    def _():
        drain(brow, rf_r)

    winv = w[...]
    pcol = [nt(bcol[s], winv) for s in range(2)]

    def update(t, c):
        panel = nt(brow[t], winv)
        first = (k == 0) & (t == 0)
        for s in range(2):
            tile = asm[s, t] - nt(panel, pcol[s])
            tile = jnp.where(first, 0.0, tile)
            if s == 0:
                tile = jnp.where(q == 0, panel, tile)
            start = t * (TILE * 4) + 2 * s
            out[pl.ds(start, TILE, stride=4), :] = tile[:, :128]
            out[pl.ds(start + 1, TILE, stride=4), :] = tile[:, 128:]
        return c

    lax.fori_loop(0, TR, update, 0)

    @pl.when(is_root)
    def _():
        ii = lax.broadcasted_iota(jnp.int32, (TILE, TILE), 0)
        jj = lax.broadcasted_iota(jnp.int32, (TILE, TILE), 1)
        factor = jnp.where(ii >= jj, u_ref[...].T, 0.0)
        out[pl.ds(0, TILE, stride=4), :] = factor[:, :128]
        out[pl.ds(1, TILE, stride=4), :] = factor[:, 128:]

    for i in range(1, NX):
        drain(stage.at[0], ch_s.at[i])

    def each(count, view, sem):
        def one(i, c):
            drain(view, sem)
            return c
        lax.fori_loop(0, count, one, 0)

    @pl.when((q == 0) & (k != 0))
    def _():
        each(jnp.where(k == NCOL, OWNERS - 1, OWNERS), brow.at[0, 0:PIECE, :], cs_s)

    each(OWNERS - 1, bcol.at[:, 0:PIECE, :], ca_s)

    @pl.when(q == 0)
    def _():
        each(NZ - 1, brow.at[:, 0:ZPIECE, :], rs_s)
        each(NZ - 1, brow.at[:, 0:ZPIECE, :], ra_s)

    @pl.when((h == 0) & (z != 0))
    def _():
        each(NZ - 2, brow.at[:, 0:ZPIECE, :], ra_s)

    @pl.when(h == 0)
    def _():
        drain(brow, rf_s)

    sent = (
        jnp.where((h == 1) & (k == 0) & (z == 0), NX - 1, 0)
        + jnp.where((h == 1) & (y == 0) & (z == 0), NY - 1, 0)
        + jnp.where((h == 1) & (z == 0), NZ - 1, 0)
        + jnp.where((h == 1) & jnp.logical_not(is_helper), 1, 0)
        + jnp.where(is_root, 1, 0)
    )
    each(sent * (NCHUNK // 2), w.at[0:NB, 0:128], w_s)
    each(sent * (NCHUNK // 2), w.at[0:NB, :], w_s)


def local(front_tiles, child_tiles, target_rows, target_cols, live_counts):
    front = front_tiles.reshape(TR * TILE * 4, 128)
    child = child_tiles.reshape(SLOTS, TILE, TILE)
    vmem = pl.BlockSpec(memory_space=pltpu.VMEM)
    smem = pl.BlockSpec(memory_space=pltpu.SMEM)
    dma = pltpu.SemaphoreType.DMA
    out = pl.pallas_call(
        kernel,
        out_shape=jax.ShapeDtypeStruct(front.shape, F32),
        in_specs=[vmem, vmem, smem, smem, smem],
        out_specs=vmem,
        scratch_shapes=[
            pltpu.VMEM((NX, STAGE_ROWS, TILE), BF16),
            pltpu.VMEM((NX, STAGE_ROWS, TILE), BF16),
            pltpu.VMEM((2, TR, TILE, TILE), F32),
            pltpu.VMEM((TR, TILE, TILE), F32),
            pltpu.VMEM((2, TILE, TILE), F32),
            pltpu.VMEM((TILE, TILE), F32),
            pltpu.VMEM((TILE, 2 * TILE), F32),
            pltpu.VMEM((TILE, TILE), F32),
            dma((NX,)), dma((NX,)),
            dma, dma((2,)),
            dma, dma,
            dma, dma,
            dma, dma((NZ,)),
            dma, dma,
            dma, dma((NCHUNK,)),
        ],
        compiler_params=pltpu.CompilerParams(
            collective_id=0, has_side_effects=True, vmem_limit_bytes=48 * 1024 * 1024
        ),
        cost_estimate=pl.CostEstimate(flops=11 * 2 * TILE**3, bytes_accessed=4 * 1024 * 1024, transcendentals=0),
        name="front_panel",
    )(front, child, target_rows.reshape(SLOTS), target_cols.reshape(SLOTS), live_counts.reshape(1))
    return out.reshape(front_tiles.shape)


def solution(mesh):
    placed = (
        P(None, ("cube", "row"), None, None, "col", None),
        P("cube", "row", "col", None, None, None),
        P("cube", "row", "col", None),
        P("cube", "row", "col", None),
        P("cube", "row", "col"),
    )
    return jax.shard_map(
        local,
        mesh=mesh,
        in_specs=placed,
        out_specs=P(None, ("cube", "row"), None, None, "col", None),
        check_vma=False,
    )
```

time: 606 us -> 69.9 us (0.12)
  waiting for transfers between devices: 457 us -> 0 us
  other arithmetic: 98.4 us -> 0 us
  Pallas kernels: 0 us -> 64.1 us
  between operations: 16 us -> 0.67 us
  matrix products: 10 us -> 0 us
  local copies, waits for them, and re-layouts: 12.6 us -> 4.9 us
  blocking collectives: 6.86 us -> 0 us
    psum x3 -> x0, waiting for transfers between devices: 425 us -> none  [from_root(): return lax.psum(kept, axis)]
    another operation x9 -> x0, other arithmetic: 93 us -> none  [the longest x3 59 us: local(): lax.linalg.triangular_solve(jnp.broadcast_to(factor, panel_raw.shape), pa...]
    pallas_call x0 -> x1, Pallas kernels: none -> 64.1 us  [local(): pl.pallas_call(kernel, out_shape=jax.ShapeDtypeStruct(front.shape, F32),...]
    all_gather x1 -> x0, waiting for transfers between devices: 31.1 us -> none  [local(): lax.all_gather(slot_values, 'cube', axis=0, tiled=True)]
    unnamed x1 -> x0, blocking collectives: 6.86 us -> none
  transfers between devices with their start and end apart: 4 -> 0, of which waited for: 4 -> 0; matrix products, arithmetic and copies ran while one was open for 1% -> 0% of each run, Pallas kernels for 0% -> 0%
where the time goes in v1:
time: 69.9 us; the launch traced here: 69.6 us
  Pallas kernels  64.1 us (92%)
  local copies, waits for them, and re-layouts  4.9 us (7%)
    pallas_call x1, Pallas kernels, local(): pl.pallas_call(kernel, out_shape=jax.ShapeDtypeStruct(front.shape, F32),...  64.1 us
    unnamed x9, local copies, waits for them, and re-layouts  4.9 us

profile of v1, /device:TPU:65, one launch (start us, length us, event | category | flops | bytes accessed | tf_op | source)
XLA Modules:
  0.0 69.6 jit_solution(8642693100324418697)
XLA Ops:
  0.7 0.0 copy-start
  0.7 1.4 %copy-done = f32[3,1,256,2,1,256]{5,4,3,2,1,0:T(1,128)S(1)} copy-done((f32[3,1,256,2,1,256]{5,4,3,2,1,0:T(1,128)S(1)}, f32[3,1,256,2,1,256]{5,4,3,2,1,0:T(1,128)}, u32[]{:S(2)}) %copy-start) | copy-done | bytes 1572888
  2.1 0.0 copy-start.1
  2.1 1.0 %copy-done.1 = bf16[1,1,1,4,256,256]{5,4,3,2,1,0:T(8,128)(2,1)S(1)} copy-done((bf16[1,1,1,4,256,256]{5,4,3,2,1,0:T(8,128)(2,1)S(1)}, bf16[1,1,1,4,256,256]{5,4,3,2,1,0:T(8,128)(2,1)}, u32[]{:S(2)}) %copy-start.1) | copy-done | bytes 524312
  3.1 0.0 copy-start.2
  3.1 0.7 copy-done.2
  3.8 0.0 copy-start.3
  3.8 0.7 copy-done.3
  4.4 64.1 %front_panel.1 = f32[3072,128]{1,0:T(8,128)S(1)} custom-call(f32[3072,128]{1,0:T(8,128)S(1)} %bitcast.8, bf16[4,256,256]{2,1,0:T(8,128)(2,1)S(1)} %bitcast.9, s32[4]{0:T(128)S(1)} %bitcast.10, s32[4]{0:T(128)S(1)} %bitcast.11, s32[1]{0:T(128)} %bitcast.6.live), custom_call_target="tpu_custom_call" | custom-call | flops 369098752 | bytes 4194304 | tf_op jit(solution)/shard_map/front_panel/pallas_call | solution.py:414
  68.5 1.1 %copy.9 = f32[3,1,256,2,1,256]{5,4,3,2,1,0:T(1,128)} copy(f32[3,1,256,2,1,256]{5,4,3,2,1,0:T(1,128)S(1)} %bitcast.7) | data formatting | bytes 3145728
Async XLA Ops:
  0.7 1.4 %copy-start = (f32[3,1,256,2,1,256]{5,4,3,2,1,0:T(1,128)S(1)}, f32[3,1,256,2,1,256]{5,4,3,2,1,0:T(1,128)}, u32[]{:S(2)}) copy-start(f32[3,1,256,2,1,256]{5,4,3,2,1,0:T(1,128)} %param.5) | copy-start | bytes 4718596
  2.1 1.0 %copy-start.1 = (bf16[1,1,1,4,256,256]{5,4,3,2,1,0:T(8,128)(2,1)S(1)}, bf16[1,1,1,4,256,256]{5,4,3,2,1,0:T(8,128)(2,1)}, u32[]{:S(2)}) copy-start(bf16[1,1,1,4,256,256]{5,4,3,2,1,0:T(8,128)(2,1)} %param.6) | copy-start | bytes 1572868
  3.1 0.7 copy-start.2
  3.8 0.7 copy-start.3

commit v2 on v1

--- a/solution.py
+++ b/solution.py
@@ -22,7 +22,9 @@
 PIECE = TILE // OWNERS
 ZPIECE = TILE // NZ
 NB = 32
-NCHUNK = TILE // NB
+NBLOCK = TILE // NB
+CHUNKS = ((0, 128, 128), (128, 64, 256), (192, 32, 256), (224, 32, 256))
+NCHUNK = len(CHUNKS)
 
 
 def nt(a, b):
@@ -37,7 +39,7 @@
 def cholesky_step(b, m_ref, u_ref, w_ref):
     row0 = pl.multiple_of(b * NB, NB)
     block = m_ref[pl.ds(row0, NB), :]
-    half = jnp.where(b < NCHUNK // 2, block[:, :128], block[:, 128:256])
+    half = jnp.where(b < NBLOCK // 2, block[:, :128], block[:, 128:256])
     diag = pltpu.roll(half, lax.rem(128 - lax.rem(b * NB, 128), 128), 1)
     parts = [block[:, 128 * i : 128 * (i + 1)] for i in range(4)] + [diag]
     rows = lax.broadcasted_iota(jnp.int32, (NB, 128), 0)
@@ -74,8 +76,8 @@
 
 
 def kernel(
-    front, child, trow, tcol, live, out,
-    stage, recv, asm, brow, bcol, w, m_ref, u_ref,
+    front_h, child_h, trow_h, tcol_h, live_h, out,
+    front, child, trow, tcol, live, in_s, stage, recv, asm, brow, bcol, w, m_ref, u_ref,
     ch_s, ch_r, cs_s, cs_r, ca_s, ca_r, rs_s, rs_r, ra_s, ra_r, rf_s, rf_r, w_s, w_r,
 ):
     x, y, q = lax.axis_index("cube"), lax.axis_index("row"), lax.axis_index("col")
@@ -84,6 +86,15 @@
     is_root = (k == 0) & (q == 0)
     is_helper = (k == 0) & (q == 1)
 
+    loads = [
+        pltpu.make_async_copy(src, dst, in_s.at[i])
+        for i, (src, dst) in enumerate(
+            [(trow_h, trow), (tcol_h, tcol), (live_h, live), (child_h, child), (front_h, front)]
+        )
+    ]
+    for load in loads:
+        load.start()
+
     def at(xx, yy, zz, hh):
         return (xx, yy, zz * 2 + hh)
 
@@ -119,6 +130,8 @@
         def _():
             greet(at(owner // NY, lax.rem(owner, NY), 0, 0))
 
+    for load in loads[:4]:
+        load.wait()
     alive = [jnp.where(m < live[0], 1, 0) for m in range(SLOTS)]
     cube_of = [lax.rem(trow[m], OWNERS) // NY for m in range(SLOTS)]
     tile_of = [(trow[m] // OWNERS) * 2 + tcol[m] // NCOL for m in range(SLOTS)]
@@ -141,6 +154,7 @@
 
     w[: TILE // 2, TILE // 2 :] = jnp.zeros((TILE // 2, TILE // 2), F32)
 
+    loads[4].wait()
     greeted_by_column = jnp.where((q != 0) | (k == 0), 0, jnp.where(k == NCOL, OWNERS - 1, OWNERS))
     pl.semaphore_wait(barrier, NX * NY - 1 + NZ - 1 + 1 + greeted_by_column)
 
@@ -176,6 +190,45 @@
 
         lax.fori_loop(0, TILE // 32, rows, 0)
 
+    def part(i):
+        row0, rows, width = CHUNKS[i]
+        return w.at[row0 : row0 + rows, 0:width]
+
+    def relay_factor():
+        for i in range(NCHUNK):
+            drain(part(i), w_r.at[i])
+
+            def pass_on(*device):
+                send(part(i), part(i), w_s, w_r.at[i], at(*device))
+
+            @pl.when(is_helper)
+            def _():
+                for j in range(1, NX):
+                    pass_on(j, 0, 0, 1)
+
+            @pl.when((y == 0) & (z == 0) & (h == 1))
+            def _():
+                for j in range(1, NY):
+                    pass_on(x, j, 0, 1)
+
+            @pl.when((z == 0) & (h == 1))
+            def _():
+                for j in range(1, NZ):
+                    pass_on(x, y, j, 1)
+
+            @pl.when((h == 1) & jnp.logical_not(is_helper))
+            def _():
+                pass_on(x, y, z, 0)
+
+    def spread_rows():
+        def spread(p, c):
+            view = pl.ds(pl.multiple_of(p * ZPIECE, ZPIECE), ZPIECE)
+            send(brow.at[:, view, :], brow.at[:, view, :], rs_s, rs_r, at(x, y, p, 0))
+            send(brow.at[:, 0:ZPIECE, :], brow.at[:, 0:ZPIECE, :], ra_s, ra_r.at[0], at(x, y, p, 0))
+            return c
+
+        lax.fori_loop(1, NZ, spread, 0)
+
     @pl.when(q == 0)
     def _():
         wait_children()
@@ -200,14 +253,11 @@
         for t in range(1, TR):
             assemble(t, 0, brow.at[t])
 
-        def spread(p, c):
-            view = pl.ds(pl.multiple_of(p * ZPIECE, ZPIECE), ZPIECE)
-            send(brow.at[:, view, :], brow.at[:, view, :], rs_s, rs_r, at(x, y, p, 0))
-            send(brow.at[:, 0:ZPIECE, :], brow.at[:, 0:ZPIECE, :], ra_s, ra_r.at[0], at(x, y, p, 0))
-            return c
-
-        lax.fori_loop(1, NZ, spread, 0)
         send(brow, brow, rf_s, rf_r, at(x, y, 0, 1))
+
+        @pl.when(k != 0)
+        def _():
+            spread_rows()
 
     @pl.when(is_root)
     def _():
@@ -217,20 +267,20 @@
         jj = lax.broadcasted_iota(jnp.int32, (TILE, TILE), 1)
         m_ref[:, TILE:] = jnp.where(ii == jj, 1.0, 0.0)
 
-        def narrow(b, c):
+        def step(b, c):
             cholesky_step(b, m_ref, u_ref, w)
-            view = pl.ds(pl.multiple_of(b * NB, NB), NB)
-            send(w.at[view, 0:128], w.at[view, 0:128], w_s, w_r.at[b], at(0, 0, 0, 1))
-            return c
-
-        def wide(b, c):
-            cholesky_step(b, m_ref, u_ref, w)
-            view = pl.ds(pl.multiple_of(b * NB, NB), NB)
-            send(w.at[view, :], w.at[view, :], w_s, w_r.at[b], at(0, 0, 0, 1))
-            return c
-
-        lax.fori_loop(0, NCHUNK // 2, narrow, 0)
-        lax.fori_loop(NCHUNK // 2, NCHUNK, wide, 0)
+            for i in range(NCHUNK):
+                @pl.when(b == (CHUNKS[i][0] + CHUNKS[i][1]) // NB - 1)
+                def _():
+                    send(part(i), part(i), w_s, w_r.at[i], at(0, 0, 0, 1))
+            return c
+
+        lax.fori_loop(0, NBLOCK, step, 0)
+
+    @pl.when(is_helper)
+    def _():
+        drain(brow, rf_r)
+        spread_rows()
 
     @pl.when(q != 0)
     def _():
@@ -263,6 +313,10 @@
 
         lax.fori_loop(1, NZ, gather_rows, 0)
 
+    @pl.when((z == 0) & (h == 1))
+    def _():
+        relay_factor()
+
     @pl.when(q != 0)
     def _():
         wait_children()
@@ -289,54 +343,13 @@
         lax.fori_loop(1, NZ, one, 0)
         send(brow, brow, rf_s, rf_r, at(x, y, z, 1))
 
-    def pass_on(b, part):
-        @pl.when((k == 0) & (z == 0))
-        def _():
-            for i in range(1, NX):
-                send(part, part, w_s, w_r.at[b], at(i, 0, 0, 1))
-
-        @pl.when((y == 0) & (z == 0))
-        def _():
-            for i in range(1, NY):
-                send(part, part, w_s, w_r.at[b], at(x, i, 0, 1))
-
-        @pl.when(z == 0)
-        def _():
-            for i in range(1, NZ):
-                send(part, part, w_s, w_r.at[b], at(x, y, i, 1))
-
-        @pl.when(jnp.logical_not(is_helper))
-        def _():
-            send(part, part, w_s, w_r.at[b], at(x, y, z, 0))
-
-    def narrow_part(b):
-        return w.at[pl.ds(pl.multiple_of(b * NB, NB), NB), 0:128]
-
-    def wide_part(b):
-        return w.at[pl.ds(pl.multiple_of(b * NB, NB), NB), :]
-
-    @pl.when(jnp.logical_not(is_root))
-    def _():
-        def narrow(b, c):
-            drain(narrow_part(b), w_r.at[b])
-            @pl.when(h == 1)
-            def _():
-                pass_on(b, narrow_part(b))
-            return c
-
-        def wide(b, c):
-            drain(wide_part(b), w_r.at[b])
-            @pl.when(h == 1)
-            def _():
-                pass_on(b, wide_part(b))
-            return c
-
-        lax.fori_loop(0, NCHUNK // 2, narrow, 0)
-        lax.fori_loop(NCHUNK // 2, NCHUNK, wide, 0)
+    @pl.when(jnp.logical_not(((z == 0) & (h == 1)) | is_root))
+    def _():
+        relay_factor()
 
     drain(bcol.at[:, 0 : TILE - PIECE, :], ca_r)
 
-    @pl.when(h == 1)
+    @pl.when((h == 1) & jnp.logical_not(is_helper))
     def _():
         drain(brow, rf_r)
 
@@ -381,7 +394,7 @@
 
     each(OWNERS - 1, bcol.at[:, 0:PIECE, :], ca_s)
 
-    @pl.when(q == 0)
+    @pl.when(((q == 0) & (k != 0)) | is_helper)
     def _():
         each(NZ - 1, brow.at[:, 0:ZPIECE, :], rs_s)
         each(NZ - 1, brow.at[:, 0:ZPIECE, :], ra_s)
@@ -401,22 +414,27 @@
         + jnp.where((h == 1) & jnp.logical_not(is_helper), 1, 0)
         + jnp.where(is_root, 1, 0)
     )
-    each(sent * (NCHUNK // 2), w.at[0:NB, 0:128], w_s)
-    each(sent * (NCHUNK // 2), w.at[0:NB, :], w_s)
+    for i in range(NCHUNK):
+        each(sent, part(i), w_s)
 
 
 def local(front_tiles, child_tiles, target_rows, target_cols, live_counts):
     front = front_tiles.reshape(TR * TILE * 4, 128)
     child = child_tiles.reshape(SLOTS, TILE, TILE)
-    vmem = pl.BlockSpec(memory_space=pltpu.VMEM)
-    smem = pl.BlockSpec(memory_space=pltpu.SMEM)
+    hbm = pl.BlockSpec(memory_space=pltpu.HBM)
     dma = pltpu.SemaphoreType.DMA
     out = pl.pallas_call(
         kernel,
-        out_shape=jax.ShapeDtypeStruct(front.shape, F32),
-        in_specs=[vmem, vmem, smem, smem, smem],
-        out_specs=vmem,
+        out_shape=pltpu.VMEM(front.shape, F32),
+        in_specs=[hbm] * 5,
+        out_specs=pl.BlockSpec(memory_space=pltpu.VMEM),
         scratch_shapes=[
+            pltpu.VMEM(front.shape, F32),
+            pltpu.VMEM(child.shape, BF16),
+            pltpu.SMEM((SLOTS,), jnp.int32),
+            pltpu.SMEM((SLOTS,), jnp.int32),
+            pltpu.SMEM((1,), jnp.int32),
+            dma((5,)),
             pltpu.VMEM((NX, STAGE_ROWS, TILE), BF16),
             pltpu.VMEM((NX, STAGE_ROWS, TILE), BF16),
             pltpu.VMEM((2, TR, TILE, TILE), F32),
@@ -434,7 +452,7 @@
             dma, dma((NCHUNK,)),
         ],
         compiler_params=pltpu.CompilerParams(
-            collective_id=0, has_side_effects=True, vmem_limit_bytes=48 * 1024 * 1024
+            collective_id=0, has_side_effects=True, vmem_limit_bytes=56 * 1024 * 1024
         ),
         cost_estimate=pl.CostEstimate(flops=11 * 2 * TILE**3, bytes_accessed=4 * 1024 * 1024, transcendentals=0),
         name="front_panel",

time: 69.9 us -> 61.4 us (0.88)
  the two profiles are of different devices: /device:TPU:65 before, /device:TPU:96 now
where the time goes in v2:
time: 61.4 us; the launch traced here: 61.3 us
  Pallas kernels  59.5 us (97%)
  local copies, waits for them, and re-layouts  1.15 us (2%)
  between operations  0.66 us (1%)
    pallas_call x1, Pallas kernels, local(): pl.pallas_call(kernel, out_shape=pltpu.VMEM(front.shape, F32), in_specs=[...  59.5 us

profile of v2, /device:TPU:96, one launch (start us, length us, event | category | flops | bytes accessed | tf_op | source)
XLA Modules:
  0.0 61.3 jit_solution(12440649651309219225)
XLA Ops:
  0.7 59.5 %front_panel.1 = f32[3072,128]{1,0:T(8,128)S(1)} custom-call(f32[3072,128]{1,0:T(8,128)} %bitcast.8, bf16[4,256,256]{2,1,0:T(8,128)(2,1)} %bitcast.9, s32[4]{0:T(128)} %bitcast.10, s32[4]{0:T(128)} %bitcast.11, s32[1]{0:T(128)} %bitcast.6.live_h), custom_call_target="tpu_custom_call" | custom-call | flops 369098752 | bytes 4194304 | tf_op jit(solution)/shard_map/front_panel/pallas_call | solution.py:426
  60.1 1.1 %copy.8 = f32[3,1,256,2,1,256]{5,4,3,2,1,0:T(1,128)} copy(f32[3,1,256,2,1,256]{5,4,3,2,1,0:T(1,128)S(1)} %bitcast.7) | data formatting | bytes 3145728

commit v3 on v2

--- a/solution.py
+++ b/solution.py
@@ -20,6 +20,7 @@
 META = LANES * TILE
 STAGE_ROWS = META + 16
 PIECE = TILE // OWNERS
+GROUP = PIECE * NY
 ZPIECE = TILE // NZ
 NB = 32
 NBLOCK = TILE // NB
@@ -28,7 +29,7 @@
 
 
 def nt(a, b):
-    return lax.dot_general(a, b, (((1,), (1,)), ((), ())), precision=HIGHEST, preferred_element_type=F32)
+    return lax.dot_general(a, b, (((1,), (1,)), ((), ())), precision=lax.Precision.HIGH, preferred_element_type=F32)
 
 
 def drain(view, sem, times=1):
@@ -78,7 +79,7 @@
 def kernel(
     front_h, child_h, trow_h, tcol_h, live_h, out,
     front, child, trow, tcol, live, in_s, stage, recv, asm, brow, bcol, w, m_ref, u_ref,
-    ch_s, ch_r, cs_s, cs_r, ca_s, ca_r, rs_s, rs_r, ra_s, ra_r, rf_s, rf_r, w_s, w_r,
+    ch_s, ch_r, cs_s, cs_r, cy_s, cy_r, cx_s, cx_r, rs_s, rs_r, ra_s, ra_r, rf_s, rf_r, w_s, w_r, go,
 ):
     x, y, q = lax.axis_index("cube"), lax.axis_index("row"), lax.axis_index("col")
     z, h = q // 2, q % 2
@@ -124,11 +125,11 @@
     lax.fori_loop(1, NZ, greet_z, 0)
     greet(at(x, y, z, 1 - h))
 
-    for s in range(2):
-        owner = s * NCOL + q
-        @pl.when((owner != 0) & jnp.logical_not((owner == k) & (q == 0)))
-        def _():
-            greet(at(owner // NY, lax.rem(owner, NY), 0, 0))
+    @pl.when((q == 0) & (my_h == 1) & (my_z != 0))
+    def _():
+        greet(at(x, y, my_z, my_h))
+
+    speaks = (my_q == q) & (q != 0)
 
     for load in loads[:4]:
         load.wait()
@@ -155,8 +156,11 @@
     w[: TILE // 2, TILE // 2 :] = jnp.zeros((TILE // 2, TILE // 2), F32)
 
     loads[4].wait()
-    greeted_by_column = jnp.where((q != 0) | (k == 0), 0, jnp.where(k == NCOL, OWNERS - 1, OWNERS))
-    pl.semaphore_wait(barrier, NX * NY - 1 + NZ - 1 + 1 + greeted_by_column)
+    pl.semaphore_wait(barrier, NX * NY - 1 + NZ - 1 + 1 + jnp.where(speaks & (h == 1) & (z != 0), 1, 0))
+
+    @pl.when(speaks)
+    def _():
+        pl.semaphore_signal(go, inc=1, device_id=at(x, y, 0, 0), device_id_type=MESH)
 
     for i in range(1, NX):
         d = lax.rem(x + i, NX)
@@ -194,8 +198,8 @@
         row0, rows, width = CHUNKS[i]
         return w.at[row0 : row0 + rows, 0:width]
 
-    def relay_factor():
-        for i in range(NCHUNK):
+    def relay_factor(first, last):
+        for i in range(first, last):
             drain(part(i), w_r.at[i])
 
             def pass_on(*device):
@@ -233,6 +237,10 @@
     def _():
         wait_children()
         assemble(0, 0, brow.at[0])
+
+        @pl.when(my_q != 0)
+        def _():
+            pl.semaphore_wait(go, 1)
 
         @pl.when(k != 0)
         def _():
@@ -291,13 +299,19 @@
         drain(bcol.at[0, 0:PIECE, :], cs_r.at[1])
 
     mine = pl.ds(pl.multiple_of(k * PIECE, PIECE), PIECE)
-
-    def gather_columns(i, c):
-        p = lax.rem(k + i, OWNERS)
-        send(bcol.at[:, mine, :], bcol.at[:, mine, :], ca_s, ca_r, at(p // NY, lax.rem(p, NY), z, h))
-        return c
-
-    lax.fori_loop(1, OWNERS, gather_columns, 0)
+    for i in range(1, NY):
+        send(bcol.at[:, mine, :], bcol.at[:, mine, :], cy_s, cy_r, at(x, lax.rem(y + i, NY), z, h))
+
+    def group(i):
+        return bcol.at[:, pl.ds(pl.multiple_of(i * GROUP, GROUP), GROUP), :]
+
+    def gather_columns():
+        drain(bcol.at[:, 0 : GROUP - PIECE, :], cy_r)
+        for i in range(1, NX):
+            send(group(x), group(x), cx_s, cx_r.at[x], at(lax.rem(x + i, NX), y, z, h))
+
+    early = (y == 0) & (z == 0) & (h == 1)
+    middle = (y != 0) & (z == 0) & (h == 1)
 
     @pl.when((h == 0) & (z != 0))
     def _():
@@ -313,9 +327,20 @@
 
         lax.fori_loop(1, NZ, gather_rows, 0)
 
-    @pl.when((z == 0) & (h == 1))
-    def _():
-        relay_factor()
+    @pl.when(early)
+    def _():
+        relay_factor(0, NCHUNK)
+        gather_columns()
+
+    @pl.when(middle)
+    def _():
+        relay_factor(0, 1)
+        gather_columns()
+        relay_factor(1, NCHUNK)
+
+    @pl.when((z != 0) | (h == 0))
+    def _():
+        gather_columns()
 
     @pl.when(q != 0)
     def _():
@@ -345,9 +370,11 @@
 
     @pl.when(jnp.logical_not(((z == 0) & (h == 1)) | is_root))
     def _():
-        relay_factor()
-
-    drain(bcol.at[:, 0 : TILE - PIECE, :], ca_r)
+        relay_factor(0, NCHUNK)
+
+    for i in range(1, NX):
+        frm = lax.rem(x + i, NX)
+        drain(group(frm), cx_r.at[frm])
 
     @pl.when((h == 1) & jnp.logical_not(is_helper))
     def _():
@@ -392,7 +419,8 @@
     def _():
         each(jnp.where(k == NCOL, OWNERS - 1, OWNERS), brow.at[0, 0:PIECE, :], cs_s)
 
-    each(OWNERS - 1, bcol.at[:, 0:PIECE, :], ca_s)
+    each(NY - 1, bcol.at[:, 0:PIECE, :], cy_s)
+    each(NX - 1, bcol.at[:, 0:GROUP, :], cx_s)
 
     @pl.when(((q == 0) & (k != 0)) | is_helper)
     def _():
@@ -446,10 +474,12 @@
             dma((NX,)), dma((NX,)),
             dma, dma((2,)),
             dma, dma,
+            dma, dma((NX,)),
             dma, dma,
             dma, dma((NZ,)),
             dma, dma,
             dma, dma((NCHUNK,)),
+            pltpu.SemaphoreType.REGULAR,
         ],
         compiler_params=pltpu.CompilerParams(
             collective_id=0, has_side_effects=True, vmem_limit_bytes=56 * 1024 * 1024

time: 61.4 us -> 58.1 us (0.946)
  the two profiles are of different devices: /device:TPU:96 before, /device:TPU:105 now
where the time goes in v3:
time: 58.1 us; the launch traced here: 57.9 us
  Pallas kernels  56.1 us (97%)
  local copies, waits for them, and re-layouts  1.15 us (2%)
  between operations  0.66 us (1%)
    pallas_call x1, Pallas kernels, local(): pl.pallas_call(kernel, out_shape=pltpu.VMEM(front.shape, F32), in_specs=[...  56.1 us

profile of v3, /device:TPU:105, one launch (start us, length us, event | category | flops | bytes accessed | tf_op | source)
XLA Modules:
  0.0 57.9 jit_solution(14845235987772203666)
XLA Ops:
  0.7 56.1 %front_panel.1 = f32[3072,128]{1,0:T(8,128)S(1)} custom-call(f32[3072,128]{1,0:T(8,128)} %bitcast.8, bf16[4,256,256]{2,1,0:T(8,128)(2,1)} %bitcast.9, s32[4]{0:T(128)} %bitcast.10, s32[4]{0:T(128)} %bitcast.11, s32[1]{0:T(128)} %bitcast.6.live_h), custom_call_target="tpu_custom_call" | custom-call | flops 369098752 | bytes 4194304 | tf_op jit(solution)/shard_map/front_panel/pallas_call | solution.py:454
  56.8 1.1 %copy.8 = f32[3,1,256,2,1,256]{5,4,3,2,1,0:T(1,128)} copy(f32[3,1,256,2,1,256]{5,4,3,2,1,0:T(1,128)S(1)} %bitcast.7) | data formatting | bytes 3145728

commit v4 on v3

--- a/solution.py
+++ b/solution.py
@@ -22,6 +22,8 @@
 PIECE = TILE // OWNERS
 GROUP = PIECE * NY
 ZPIECE = TILE // NZ
+CODED_ROWS = TR * ZPIECE + 16
+LIMIT, STEPS = 80.0, 32767.0
 NB = 32
 NBLOCK = TILE // NB
 CHUNKS = ((0, 128, 128), (128, 64, 256), (192, 32, 256), (224, 32, 256))
@@ -78,7 +80,7 @@
 
 def kernel(
     front_h, child_h, trow_h, tcol_h, live_h, out,
-    front, child, trow, tcol, live, in_s, stage, recv, asm, brow, bcol, w, m_ref, u_ref,
+    front, child, trow, tcol, live, in_s, stage, recv, asm, brow, coded, bcol, w, m_ref, u_ref,
     ch_s, ch_r, cs_s, cs_r, cy_s, cy_r, cx_s, cx_r, rs_s, rs_r, ra_s, ra_r, rf_s, rf_r, w_s, w_r, go,
 ):
     x, y, q = lax.axis_index("cube"), lax.axis_index("row"), lax.axis_index("col")
@@ -224,11 +226,46 @@
             def _():
                 pass_on(x, y, z, 0)
 
+    def encode(v):
+        return ((v + (STEPS + 1.5)).astype(jnp.int32) - int(STEPS + 1)).astype(jnp.int16)
+
+    def encode_rows():
+        tag_row = lax.broadcasted_iota(jnp.int32, (16, TILE), 0)
+        tags = jnp.zeros((16, TILE), F32)
+        inverse = []
+        for t in range(TR):
+            peak = jnp.max(jnp.max(jnp.abs(brow[t]), axis=0, keepdims=True), axis=1, keepdims=True)
+            level = jnp.floor(peak * (STEPS / LIMIT)) + 1.0
+            level = jnp.broadcast_to(level, (1, TILE))
+            tags = jnp.where(tag_row == t, level, tags)
+            inverse.append((STEPS * STEPS / LIMIT) / level)
+
+        def one(p, c):
+            view = pl.ds(pl.multiple_of(p * ZPIECE, ZPIECE), ZPIECE)
+            for t in range(TR):
+                coded[p, t * ZPIECE : (t + 1) * ZPIECE, :] = encode(brow[t, view, :] * inverse[t])
+            coded[p, TR * ZPIECE :, :] = tags.astype(jnp.int32).astype(jnp.int16)
+            return c
+
+        lax.fori_loop(0, NZ, one, 0)
+
+    def decode_rows():
+        def one(p, c):
+            view = pl.ds(pl.multiple_of(p * ZPIECE, ZPIECE), ZPIECE)
+            tags = coded[p, TR * ZPIECE :, :].astype(jnp.int32).astype(F32) * (LIMIT / (STEPS * STEPS))
+            for t in range(TR):
+                v = coded[p, t * ZPIECE : (t + 1) * ZPIECE, :].astype(jnp.int32).astype(F32)
+                brow[t, view, :] = v * tags[t : t + 1, :]
+            return c
+
+        lax.fori_loop(0, NZ, one, 0)
+
     def spread_rows():
+        encode_rows()
+
         def spread(p, c):
-            view = pl.ds(pl.multiple_of(p * ZPIECE, ZPIECE), ZPIECE)
-            send(brow.at[:, view, :], brow.at[:, view, :], rs_s, rs_r, at(x, y, p, 0))
-            send(brow.at[:, 0:ZPIECE, :], brow.at[:, 0:ZPIECE, :], ra_s, ra_r.at[0], at(x, y, p, 0))
+            send(coded.at[p], coded.at[p], rs_s, rs_r, at(x, y, p, 0))
+            send(coded.at[0], coded.at[0], ra_s, ra_r.at[0], at(x, y, p, 0))
             return c
 
         lax.fori_loop(1, NZ, spread, 0)
@@ -315,14 +352,13 @@
 
     @pl.when((h == 0) & (z != 0))
     def _():
-        drain(brow.at[:, 0:ZPIECE, :], rs_r)
-        view = pl.ds(pl.multiple_of(z * ZPIECE, ZPIECE), ZPIECE)
+        drain(coded.at[0], rs_r)
 
         def gather_rows(i, c):
             to = lax.rem(z + i, NZ)
             @pl.when(to != 0)
             def _():
-                send(brow.at[:, view, :], brow.at[:, view, :], ra_s, ra_r.at[z], at(x, y, to, 0))
+                send(coded.at[z], coded.at[z], ra_s, ra_r.at[z], at(x, y, to, 0))
             return c
 
         lax.fori_loop(1, NZ, gather_rows, 0)
@@ -362,11 +398,12 @@
     def _():
         def one(i, c):
             frm = lax.rem(z + i, NZ)
-            drain(brow.at[:, 0:ZPIECE, :], ra_r.at[frm])
+            drain(coded.at[0], ra_r.at[frm])
             return c
 
         lax.fori_loop(1, NZ, one, 0)
-        send(brow, brow, rf_s, rf_r, at(x, y, z, 1))
+        send(coded, coded, rf_s, rf_r, at(x, y, z, 1))
+        decode_rows()
 
     @pl.when(jnp.logical_not(((z == 0) & (h == 1)) | is_root))
     def _():
@@ -376,9 +413,14 @@
         frm = lax.rem(x + i, NX)
         drain(group(frm), cx_r.at[frm])
 
-    @pl.when((h == 1) & jnp.logical_not(is_helper))
+    @pl.when((q == 1) & (k != 0))
     def _():
         drain(brow, rf_r)
+
+    @pl.when((h == 1) & (z != 0))
+    def _():
+        drain(coded, rf_r)
+        decode_rows()
 
     winv = w[...]
     pcol = [nt(bcol[s], winv) for s in range(2)]
@@ -424,14 +466,15 @@
 
     @pl.when(((q == 0) & (k != 0)) | is_helper)
     def _():
-        each(NZ - 1, brow.at[:, 0:ZPIECE, :], rs_s)
-        each(NZ - 1, brow.at[:, 0:ZPIECE, :], ra_s)
+        each(NZ - 1, coded.at[0], rs_s)
+        each(NZ - 1, coded.at[0], ra_s)
 
     @pl.when((h == 0) & (z != 0))
     def _():
-        each(NZ - 2, brow.at[:, 0:ZPIECE, :], ra_s)
-
-    @pl.when(h == 0)
+        each(NZ - 2, coded.at[0], ra_s)
+        drain(coded, rf_s)
+
+    @pl.when(q == 0)
     def _():
         drain(brow, rf_s)
 
@@ -467,6 +510,7 @@
             pltpu.VMEM((NX, STAGE_ROWS, TILE), BF16),
             pltpu.VMEM((2, TR, TILE, TILE), F32),
             pltpu.VMEM((TR, TILE, TILE), F32),
+            pltpu.VMEM((NZ, CODED_ROWS, TILE), jnp.int16),
             pltpu.VMEM((2, TILE, TILE), F32),
             pltpu.VMEM((TILE, TILE), F32),
             pltpu.VMEM((TILE, 2 * TILE), F32),

time: 58.1 us -> 52.7 us (0.907)
  the two profiles are of different devices: /device:TPU:105 before, /device:TPU:1 now
where the time goes in v4:
time: 52.7 us; the launch traced here: 52.6 us
  Pallas kernels  50.8 us (96%)
  local copies, waits for them, and re-layouts  1.15 us (2%)
  between operations  0.66 us (1%)
    pallas_call x1, Pallas kernels, local(): pl.pallas_call(kernel, out_shape=pltpu.VMEM(front.shape, F32), in_specs=[...  50.8 us
    unnamed x1, local copies, waits for them, and re-layouts  1.15 us

profile of v4, /device:TPU:1, one launch (start us, length us, event | category | flops | bytes accessed | tf_op | source)
XLA Modules:
  0.0 52.6 jit_solution(10163302555911852843)
XLA Ops:
  0.7 50.8 %front_panel.1 = f32[3072,128]{1,0:T(8,128)S(1)} custom-call(f32[3072,128]{1,0:T(8,128)} %bitcast.8, bf16[4,256,256]{2,1,0:T(8,128)(2,1)} %bitcast.9, s32[4]{0:T(128)} %bitcast.10, s32[4]{0:T(128)} %bitcast.11, s32[1]{0:T(128)} %bitcast.6.live_h), custom_call_target="tpu_custom_call" | custom-call | flops 369098752 | bytes 4194304 | tf_op jit(solution)/shard_map/front_panel/pallas_call | solution.py:497
  51.4 1.1 %copy.8 = f32[3,1,256,2,1,256]{5,4,3,2,1,0:T(1,128)} copy(f32[3,1,256,2,1,256]{5,4,3,2,1,0:T(1,128)S(1)} %bitcast.7) | data formatting | bytes 3145728

commit v5 on v4

--- a/solution.py
+++ b/solution.py
@@ -19,13 +19,17 @@
 LANES = 2
 META = LANES * TILE
 STAGE_ROWS = META + 16
-PIECE = TILE // OWNERS
+PIECE = 2 * TILE // OWNERS
 GROUP = PIECE * NY
+HALF = TILE // 2
 ZPIECE = TILE // NZ
 CODED_ROWS = TR * ZPIECE + 16
 LIMIT, STEPS = 80.0, 32767.0
 NB = 32
 NBLOCK = TILE // NB
+AWAY_X = list(range(1, NX))
+AWAY_Y = list(range(1, NY))
+AWAY_Z = list(range(1, NZ))
 CHUNKS = ((0, 128, 128), (128, 64, 256), (192, 32, 256), (224, 32, 256))
 NCHUNK = len(CHUNKS)
 
@@ -44,30 +48,36 @@
     block = m_ref[pl.ds(row0, NB), :]
     half = jnp.where(b < NBLOCK // 2, block[:, :128], block[:, 128:256])
     diag = pltpu.roll(half, lax.rem(128 - lax.rem(b * NB, 128), 128), 1)
-    parts = [block[:, 128 * i : 128 * (i + 1)] for i in range(4)] + [diag]
-    rows = lax.broadcasted_iota(jnp.int32, (NB, 128), 0)
+    left = b < NBLOCK // 2
+    shared = jnp.where(left, block[:, :128], block[:, 384:])
+    parts = [shared, block[:, 128:256], block[:, 256:384], diag]
+    first_rows = lax.broadcasted_iota(jnp.int32, (8, 128), 0)
+    done = [[] for _ in parts]
     for g in range(NB // 8):
-        base = 8 * g
-        cols = [jnp.broadcast_to(parts[4][base:, base + j : base + j + 1], (NB - base, 128)) for j in range(8)]
-        live = [p[base:] for p in parts]
-        below = rows[base:] - base
+        more = NB - 8 * g - 8
+        cols = [jnp.broadcast_to(parts[3][:, 8 * g + j : 8 * g + j + 1], (more + 8, 128)) for j in range(8)]
+        head = [p[:8] for p in parts]
+        tail = [p[8:] for p in parts]
         for kk in range(8):
             pivot = cols[kk][kk : kk + 1, :]
             inv = lax.rsqrt(pivot)
-            inv = inv * (1.5 - 0.5 * pivot * inv * inv)
             col = cols[kk] * inv
-            masked = jnp.where(below > kk, col, 0.0)
             for j in range(kk + 1, 8):
-                cols[j] = cols[j] - masked * col[j : j + 1, :]
-            for i in range(5):
-                top = live[i][kk : kk + 1, :] * inv
-                live[i] = jnp.where(below == kk, top, live[i] - masked * top)
-        parts = [l if g == 0 else jnp.concatenate([p[:base], l], axis=0) for p, l in zip(parts, live)]
-    u = jnp.concatenate(parts[:2], axis=1)
-    winv = jnp.concatenate(parts[2:4], axis=1)
-    u_ref[pl.ds(row0, NB), :] = u
-    w_ref[pl.ds(row0, NB), :] = winv
-    both = jnp.concatenate(parts[:4], axis=1)
+                cols[j] = cols[j] - col * col[j : j + 1, :]
+            masked = jnp.where(first_rows > kk, col[:8], 0.0)
+            for i in range(len(parts)):
+                top = head[i][kk : kk + 1, :] * inv
+                head[i] = jnp.where(first_rows == kk, top, head[i] - masked * top)
+                if more:
+                    tail[i] = tail[i] - col[8:] * top
+        for i in range(len(parts)):
+            done[i].append(head[i])
+        parts = tail
+    shared, u_right, w_left = [jnp.concatenate(d, axis=0) for d in done[:3]]
+    zero = jnp.zeros_like(shared)
+    both = jnp.concatenate([jnp.where(left, shared, zero), u_right, w_left, jnp.where(left, zero, shared)], axis=1)
+    u_ref[pl.ds(row0, NB), :] = both[:, :TILE]
+    w_ref[pl.ds(row0, NB), :] = both[:, TILE:]
     b1 = both.astype(BF16)
     rest = both - b1.astype(F32)
     b2 = rest.astype(BF16)
@@ -80,7 +90,7 @@
 
 def kernel(
     front_h, child_h, trow_h, tcol_h, live_h, out,
-    front, child, trow, tcol, live, in_s, stage, recv, asm, brow, coded, bcol, w, m_ref, u_ref,
+    front, child, trow, tcol, live, in_s, stage, recv, asm, brow, coded, col_out, col_in, col, bcol, w, m_ref, u_ref,
     ch_s, ch_r, cs_s, cs_r, cy_s, cy_r, cx_s, cx_r, rs_s, rs_r, ra_s, ra_r, rf_s, rf_r, w_s, w_r, go,
 ):
     x, y, q = lax.axis_index("cube"), lax.axis_index("row"), lax.axis_index("col")
@@ -164,7 +174,7 @@
     def _():
         pl.semaphore_signal(go, inc=1, device_id=at(x, y, 0, 0), device_id_type=MESH)
 
-    for i in range(1, NX):
+    for i in AWAY_X:
         d = lax.rem(x + i, NX)
         send(stage.at[d], recv.at[x], ch_s.at[i], ch_r.at[x], at(d, y, z, h))
     recv[x] = stage[x]
@@ -209,17 +219,17 @@
 
             @pl.when(is_helper)
             def _():
-                for j in range(1, NX):
+                for j in AWAY_X:
                     pass_on(j, 0, 0, 1)
 
             @pl.when((y == 0) & (z == 0) & (h == 1))
             def _():
-                for j in range(1, NY):
+                for j in AWAY_Y:
                     pass_on(x, j, 0, 1)
 
             @pl.when((z == 0) & (h == 1))
             def _():
-                for j in range(1, NZ):
+                for j in AWAY_Z:
                     pass_on(x, y, j, 1)
 
             @pl.when((h == 1) & jnp.logical_not(is_helper))
@@ -228,15 +238,40 @@
 
     def encode(v):
         return ((v + (STEPS + 1.5)).astype(jnp.int32) - int(STEPS + 1)).astype(jnp.int16)
+
+    def level_of(t):
+        peak = jnp.max(jnp.max(jnp.abs(brow[t]), axis=0, keepdims=True), axis=1, keepdims=True)
+        return jnp.broadcast_to(jnp.floor(peak * (STEPS / LIMIT)) + 1.0, (1, TILE))
+
+    def encode_column():
+        level = level_of(0)[:, :HALF]
+        inverse = (STEPS * STEPS / LIMIT) / level
+        tags = jnp.broadcast_to(level, (PIECE, HALF)).astype(jnp.int32).astype(jnp.int16)
+
+        def one(i, c):
+            view = pl.ds(pl.multiple_of(i * PIECE, PIECE), PIECE)
+            for side in range(2):
+                at_piece = side * (OWNERS // 2) + i
+                v = brow[0, view, side * HALF : (side + 1) * HALF]
+                col_out[at_piece, 0:PIECE, :] = encode(v * inverse)
+                col_out[at_piece, PIECE:, :] = tags
+            return c
+
+        lax.fori_loop(0, OWNERS // 2, one, 0)
+
+    def decode_columns():
+        for s in range(2):
+            tags = col_in[s, PIECE:, :].astype(jnp.int32).astype(F32)[0:1, :] * (LIMIT / (STEPS * STEPS))
+            for side in range(2):
+                v = col[s, side * TILE : (side + 1) * TILE, :].astype(jnp.int32).astype(F32)
+                bcol[s, :, side * HALF : (side + 1) * HALF] = v * tags
 
     def encode_rows():
         tag_row = lax.broadcasted_iota(jnp.int32, (16, TILE), 0)
         tags = jnp.zeros((16, TILE), F32)
         inverse = []
         for t in range(TR):
-            peak = jnp.max(jnp.max(jnp.abs(brow[t]), axis=0, keepdims=True), axis=1, keepdims=True)
-            level = jnp.floor(peak * (STEPS / LIMIT)) + 1.0
-            level = jnp.broadcast_to(level, (1, TILE))
+            level = level_of(t)
             tags = jnp.where(tag_row == t, level, tags)
             inverse.append((STEPS * STEPS / LIMIT) / level)
 
@@ -263,17 +298,18 @@
     def spread_rows():
         encode_rows()
 
-        def spread(p, c):
+        for p in AWAY_Z:
             send(coded.at[p], coded.at[p], rs_s, rs_r, at(x, y, p, 0))
+        for p in AWAY_Z:
             send(coded.at[0], coded.at[0], ra_s, ra_r.at[0], at(x, y, p, 0))
-            return c
-
-        lax.fori_loop(1, NZ, spread, 0)
 
     @pl.when(q == 0)
     def _():
         wait_children()
         assemble(0, 0, brow.at[0])
+        @pl.when(k != 0)
+        def _():
+            encode_column()
 
         @pl.when(my_q != 0)
         def _():
@@ -282,10 +318,9 @@
         @pl.when(k != 0)
         def _():
             def scatter(p, c):
-                view = pl.ds(pl.multiple_of(p * PIECE, PIECE), PIECE)
                 @pl.when((p != k) | (my_q != 0))
                 def _():
-                    send(brow.at[0, view, :], bcol.at[my_s, view, :], cs_s, cs_r.at[my_s],
+                    send(col_out.at[p], col_in.at[my_s], cs_s, cs_r.at[my_s],
                          at(p // NY, lax.rem(p, NY), my_z, my_h))
                 return c
 
@@ -293,7 +328,7 @@
 
         @pl.when(k == NCOL)
         def _():
-            bcol[1, NCOL * PIECE : (NCOL + 1) * PIECE, :] = brow[0, NCOL * PIECE : (NCOL + 1) * PIECE, :]
+            col_in[1] = col_out[NCOL]
 
         for t in range(1, TR):
             assemble(t, 0, brow.at[t])
@@ -329,22 +364,24 @@
 
     @pl.when(q != 0)
     def _():
-        drain(bcol.at[0, 0:PIECE, :], cs_r.at[0])
+        drain(col_in.at[0], cs_r.at[0])
 
     @pl.when(jnp.logical_not((q == 0) & (k == NCOL)))
     def _():
-        drain(bcol.at[0, 0:PIECE, :], cs_r.at[1])
+        drain(col_in.at[1], cs_r.at[1])
 
     mine = pl.ds(pl.multiple_of(k * PIECE, PIECE), PIECE)
-    for i in range(1, NY):
-        send(bcol.at[:, mine, :], bcol.at[:, mine, :], cy_s, cy_r, at(x, lax.rem(y + i, NY), z, h))
+    for s in range(2):
+        col[s, mine, :] = col_in[s, 0:PIECE, :]
+    for i in AWAY_Y:
+        send(col.at[:, mine, :], col.at[:, mine, :], cy_s, cy_r, at(x, lax.rem(y + i, NY), z, h))
 
     def group(i):
-        return bcol.at[:, pl.ds(pl.multiple_of(i * GROUP, GROUP), GROUP), :]
+        return col.at[:, pl.ds(pl.multiple_of(i * GROUP, GROUP), GROUP), :]
 
     def gather_columns():
-        drain(bcol.at[:, 0 : GROUP - PIECE, :], cy_r)
-        for i in range(1, NX):
+        drain(col.at[:, 0 : GROUP - PIECE, :], cy_r)
+        for i in AWAY_X:
             send(group(x), group(x), cx_s, cx_r.at[x], at(lax.rem(x + i, NX), y, z, h))
 
     early = (y == 0) & (z == 0) & (h == 1)
@@ -354,14 +391,11 @@
     def _():
         drain(coded.at[0], rs_r)
 
-        def gather_rows(i, c):
+        for i in AWAY_Z:
             to = lax.rem(z + i, NZ)
             @pl.when(to != 0)
             def _():
                 send(coded.at[z], coded.at[z], ra_s, ra_r.at[z], at(x, y, to, 0))
-            return c
-
-        lax.fori_loop(1, NZ, gather_rows, 0)
 
     @pl.when(early)
     def _():
@@ -412,6 +446,7 @@
     for i in range(1, NX):
         frm = lax.rem(x + i, NX)
         drain(group(frm), cx_r.at[frm])
+    decode_columns()
 
     @pl.when((q == 1) & (k != 0))
     def _():
@@ -459,10 +494,10 @@
 
     @pl.when((q == 0) & (k != 0))
     def _():
-        each(jnp.where(k == NCOL, OWNERS - 1, OWNERS), brow.at[0, 0:PIECE, :], cs_s)
-
-    each(NY - 1, bcol.at[:, 0:PIECE, :], cy_s)
-    each(NX - 1, bcol.at[:, 0:GROUP, :], cx_s)
+        each(jnp.where(k == NCOL, OWNERS - 1, OWNERS), col_out.at[0], cs_s)
+
+    each(NY - 1, col.at[:, 0:PIECE, :], cy_s)
+    each(NX - 1, col.at[:, 0:GROUP, :], cx_s)
 
     @pl.when(((q == 0) & (k != 0)) | is_helper)
     def _():
@@ -511,6 +546,9 @@
             pltpu.VMEM((2, TR, TILE, TILE), F32),
             pltpu.VMEM((TR, TILE, TILE), F32),
             pltpu.VMEM((NZ, CODED_ROWS, TILE), jnp.int16),
+            pltpu.VMEM((OWNERS, 2 * PIECE, HALF), jnp.int16),
+            pltpu.VMEM((2, 2 * PIECE, HALF), jnp.int16),
+            pltpu.VMEM((2, 2 * TILE, HALF), jnp.int16),
             pltpu.VMEM((2, TILE, TILE), F32),
             pltpu.VMEM((TILE, TILE), F32),
             pltpu.VMEM((TILE, 2 * TILE), F32),

time: 52.7 us -> 51.9 us (0.985)
  the two profiles are of different devices: /device:TPU:1 before, /device:TPU:94 now
where the time goes in v5:
time: 51.9 us; the launch traced here: 51.8 us
  Pallas kernels  50 us (96%)
  local copies, waits for them, and re-layouts  1.15 us (2%)
  between operations  0.66 us (1%)
    pallas_call x1, Pallas kernels, local(): pl.pallas_call(kernel, out_shape=pltpu.VMEM(front.shape, F32), in_specs=[...  50 us
    unnamed x1, local copies, waits for them, and re-layouts  1.15 us

profile of v5, /device:TPU:94, one launch (start us, length us, event | category | flops | bytes accessed | tf_op | source)
XLA Modules:
  0.0 51.8 jit_solution(5047481809148498694)
XLA Ops:
  0.7 50.0 %front_panel.1 = f32[3072,128]{1,0:T(8,128)S(1)} custom-call(f32[3072,128]{1,0:T(8,128)} %bitcast.8, bf16[4,256,256]{2,1,0:T(8,128)(2,1)} %bitcast.9, s32[4]{0:T(128)} %bitcast.10, s32[4]{0:T(128)} %bitcast.11, s32[1]{0:T(128)} %bitcast.6.live_h), custom_call_target="tpu_custom_call" | custom-call | flops 369098752 | bytes 4194304 | tf_op jit(solution)/shard_map/front_panel/pallas_call | solution.py:532
  50.6 1.1 %copy.8 = f32[3,1,256,2,1,256]{5,4,3,2,1,0:T(1,128)} copy(f32[3,1,256,2,1,256]{5,4,3,2,1,0:T(1,128)S(1)} %bitcast.7) | data formatting | bytes 3145728

commit v6 on v5

--- a/solution.py
+++ b/solution.py
@@ -30,7 +30,7 @@
 AWAY_X = list(range(1, NX))
 AWAY_Y = list(range(1, NY))
 AWAY_Z = list(range(1, NZ))
-CHUNKS = ((0, 128, 128), (128, 64, 256), (192, 32, 256), (224, 32, 256))
+CHUNKS = ((0, 128, 128), (128, 32, 256), (160, 32, 256), (192, 32, 256), (224, 32, 256))
 NCHUNK = len(CHUNKS)
 
 
@@ -217,11 +217,6 @@
             def pass_on(*device):
                 send(part(i), part(i), w_s, w_r.at[i], at(*device))
 
-            @pl.when(is_helper)
-            def _():
-                for j in AWAY_X:
-                    pass_on(j, 0, 0, 1)
-
             @pl.when((y == 0) & (z == 0) & (h == 1))
             def _():
                 for j in AWAY_Y:
@@ -352,7 +347,8 @@
             for i in range(NCHUNK):
                 @pl.when(b == (CHUNKS[i][0] + CHUNKS[i][1]) // NB - 1)
                 def _():
-                    send(part(i), part(i), w_s, w_r.at[i], at(0, 0, 0, 1))
+                    for j in range(NX):
+                        send(part(i), part(i), w_s, w_r.at[i], at(j, 0, 0, 1))
             return c
 
         lax.fori_loop(0, NBLOCK, step, 0)
@@ -404,9 +400,9 @@
 
     @pl.when(middle)
     def _():
-        relay_factor(0, 1)
+        relay_factor(0, 2)
         gather_columns()
-        relay_factor(1, NCHUNK)
+        relay_factor(2, NCHUNK)
 
     @pl.when((z != 0) | (h == 0))
     def _():
@@ -439,14 +435,23 @@
         send(coded, coded, rf_s, rf_r, at(x, y, z, 1))
         decode_rows()
 
+    def finish_columns():
+        for i in range(1, NX):
+            frm = lax.rem(x + i, NX)
+            drain(group(frm), cx_r.at[frm])
+        decode_columns()
+
+    @pl.when(h == 0)
+    def _():
+        finish_columns()
+
     @pl.when(jnp.logical_not(((z == 0) & (h == 1)) | is_root))
     def _():
         relay_factor(0, NCHUNK)
 
-    for i in range(1, NX):
-        frm = lax.rem(x + i, NX)
-        drain(group(frm), cx_r.at[frm])
-    decode_columns()
+    @pl.when(h == 1)
+    def _():
+        finish_columns()
 
     @pl.when((q == 1) & (k != 0))
     def _():
@@ -514,11 +519,10 @@
         drain(brow, rf_s)
 
     sent = (
-        jnp.where((h == 1) & (k == 0) & (z == 0), NX - 1, 0)
-        + jnp.where((h == 1) & (y == 0) & (z == 0), NY - 1, 0)
+        jnp.where((h == 1) & (y == 0) & (z == 0), NY - 1, 0)
         + jnp.where((h == 1) & (z == 0), NZ - 1, 0)
         + jnp.where((h == 1) & jnp.logical_not(is_helper), 1, 0)
-        + jnp.where(is_root, 1, 0)
+        + jnp.where(is_root, NX, 0)
     )
     for i in range(NCHUNK):
         each(sent, part(i), w_s)

time: 51.9 us -> 51.8 us (level)
  the two profiles are of different devices: /device:TPU:94 before, /device:TPU:65 now
where the time goes in v6:
time: 51.8 us; the launch traced here: 51.2 us
  Pallas kernels  49.4 us (95%)
  local copies, waits for them, and re-layouts  1.15 us (2%)
  between operations  0.66 us (1%)
    pallas_call x1, Pallas kernels, local(): pl.pallas_call(kernel, out_shape=pltpu.VMEM(front.shape, F32), in_specs=[...  49.4 us
    unnamed x1, local copies, waits for them, and re-layouts  1.15 us

profile of v6, /device:TPU:65, one launch (start us, length us, event | category | flops | bytes accessed | tf_op | source)
XLA Modules:
  0.0 51.2 jit_solution(7771328490003801665)
XLA Ops:
  0.7 49.4 %front_panel.1 = f32[3072,128]{1,0:T(8,128)S(1)} custom-call(f32[3072,128]{1,0:T(8,128)} %bitcast.8, bf16[4,256,256]{2,1,0:T(8,128)(2,1)} %bitcast.9, s32[4]{0:T(128)} %bitcast.10, s32[4]{0:T(128)} %bitcast.11, s32[1]{0:T(128)} %bitcast.6.live_h), custom_call_target="tpu_custom_call" | custom-call | flops 369098752 | bytes 4194304 | tf_op jit(solution)/shard_map/front_panel/pallas_call | solution.py:536
  50.1 1.1 %copy.8 = f32[3,1,256,2,1,256]{5,4,3,2,1,0:T(1,128)} copy(f32[3,1,256,2,1,256]{5,4,3,2,1,0:T(1,128)S(1)} %bitcast.7) | data formatting | bytes 3145728
